TPU v7x, 32 devices: a whole 2x2x4 slice. The times are simulated.
32 devices in a mesh: band: 8 (over y, x, core), req: 4 (over z).
Axes of the slice: x: 2, y: 2, z: 4, core: 2. Of those that a mesh axis runs over, the one named last changes fastest.
Arguments:
- latents: bfloat16 [4, 32, 512, 320], P('req', 'band'), may hold values from -40 to 40
- request_time_embedding: bfloat16 [4, 1280], P('req'), may hold values from -6 to 6
- request_adapter: int32 [4, 1], P('req'), may hold values from 0 to 31, as said below
- adapter_stored_row: int32 [32], replicated, may hold values from 0 to 31, as said below
- first_conv_weight: bfloat16 [3, 3, 320, 320], replicated, may hold values from -0.109375 to 0.109375
- stored_down_weight: bfloat16 [32, 3, 3, 320, 64], P(('band', 'req')), may hold values from -0.109375 to 0.109375
- stored_up_weight: bfloat16 [32, 64, 320], P(('band', 'req')), may hold values from -0.75 to 0.75
- second_conv_weight: bfloat16 [3, 3, 320, 320], replicated, may hold values from -0.109375 to 0.109375
- time_projection_weight: bfloat16 [1280, 320], replicated, may hold values from -0.15625 to 0.15625
Outputs:
- block_out: bfloat16 [4, 32, 512, 320], P('req', 'band')
Inputs may be any that keep to these rules, and one draw needn't show every extreme that they name: `request_adapter`: ids of adapters. `adapter_stored_row`: each stored row appears once.
All inputs are finite; a program needn't handle non-finite values.
Results may differ from a plain program's by a relative error of at most 0.0038.
Values may be sent and summed in bfloat16 or wider, within the bound.
A program may use at most 128 MiB of HBM per device.

v0:
```python
import jax
import jax.numpy as jnp
from jax import lax
from jax.sharding import PartitionSpec as P

G = 32


def with_halo(x, sides, width):
    for axis, dim in sides:
        count, length = (lax.axis_size(axis), x.shape[dim])
        up = [(i, (i + 1) % count) for i in range(count - 1)]
        down = [(j, i) for i, j in up]
        last = lax.slice_in_dim(x, length - width, length, axis=dim)
        initial = lax.slice_in_dim(x, 0, width, axis=dim)
        before = lax.ppermute(last, axis, up)
        after = lax.ppermute(initial, axis, down)
        x = jnp.concatenate([before, x, after], axis=dim)
    return x


def group_norm(field, groups, total_rows):
    requests, rows, width, channels = field.shape
    grouped = field.reshape(requests, rows, width, groups, channels // groups)
    count = total_rows * width * (channels // groups)
    sums = lax.psum(jnp.sum(grouped, axis=(1, 2, 4)), "band")
    center = (sums / count)[:, None, None, :, None]
    deviation = grouped - center
    spread = lax.psum(jnp.sum(deviation * deviation, axis=(1, 2, 4)), "band") / count
    normed = deviation * lax.rsqrt(spread + 1e-05)[:, None, None, :, None]
    return normed.reshape(field.shape)


def padded_field(field):
    extended = with_halo(field, (("band", 1),), 1)
    return jnp.pad(extended, ((0, 0), (0, 0), (1, 1), (0, 0)))


def convolve(padded, kernel, rows, width):
    total = None
    for row_tap in range(3):
        for col_tap in range(3):
            term = jnp.einsum(
                "qhwc,cd->qhwd",
                padded[:, row_tap : row_tap + rows, col_tap : col_tap + width],
                kernel[row_tap, col_tap],
                preferred_element_type=jnp.float32,
            )
            total = term if total is None else total + term
    return total


def convolve_each(padded, kernels, rows, width):
    total = None
    for row_tap in range(3):
        for col_tap in range(3):
            term = jnp.einsum(
                "qhwc,qcd->qhwd",
                padded[:, row_tap : row_tap + rows, col_tap : col_tap + width],
                kernels[:, row_tap, col_tap],
                preferred_element_type=jnp.float32,
            )
            total = term if total is None else total + term
    return total


def select_rows(slots, to_global, pieces):
    down_piece, up_piece = pieces
    count = down_piece.shape[0]
    stored = to_global(jnp.arange(count, dtype=jnp.int32))
    matches = stored[None, :] == slots[:, None]
    zero = jnp.zeros((), down_piece.dtype)
    down_pick = jnp.sum(
        jnp.where(matches[:, :, None, None, None, None], down_piece[None], zero), axis=1
    )
    up_pick = jnp.sum(jnp.where(matches[:, :, None, None], up_piece[None], zero), axis=1)
    return (down_pick, up_pick)


def slots_of(adapter_ids, adapter_stored_row):
    adapter_count = adapter_stored_row.shape[0]
    picked = adapter_ids == jnp.arange(adapter_count, dtype=jnp.int32)[None, :]
    return jnp.sum(jnp.where(picked, adapter_stored_row[None, :], 0), axis=1)


def shards(
    latents,
    request_time_embedding,
    request_adapter,
    adapter_stored_row,
    first_conv_weight,
    stored_down_weight,
    stored_up_weight,
    second_conv_weight,
    time_projection_weight,
):
    requests, rows, width, channels = latents.shape
    total_rows = rows * lax.axis_size("band")
    held_adapters = stored_down_weight.shape[0]
    req_count = lax.axis_size("req")
    slots = slots_of(request_adapter, adapter_stored_row)
    band_base = lax.axis_index("band") * (req_count * held_adapters)

    def column_global(gathered):
        return band_base + gathered

    part_down, part_up = select_rows(
        slots,
        column_global,
        (
            lax.all_gather(stored_down_weight, "req", axis=0, tiled=True),
            lax.all_gather(stored_up_weight, "req", axis=0, tiled=True),
        ),
    )
    sum_down, sum_up = (
        lax.psum(part_down, "band").astype(jnp.float32),
        lax.psum(part_up, "band").astype(jnp.float32),
    )
    chosen_down = sum_down.astype(jnp.bfloat16)
    chosen_up = sum_up.astype(jnp.bfloat16)
    shift = jnp.dot(
        jax.nn.silu(request_time_embedding.astype(jnp.float32)).astype(jnp.bfloat16),
        time_projection_weight,
        preferred_element_type=jnp.float32,
    )
    groups = G
    first = jax.nn.silu(group_norm(latents.astype(jnp.float32), groups, total_rows)).astype(
        jnp.bfloat16
    )
    first_padded = padded_field(first)
    main = convolve(first_padded, first_conv_weight, rows, width)
    lowrank = convolve_each(first_padded, chosen_down, rows, width).astype(jnp.bfloat16)
    lifted = jnp.einsum("qhwk,qkc->qhwc", lowrank, chosen_up, preferred_element_type=jnp.float32)
    hidden = main + lifted + shift[:, None, None, :]
    second = jax.nn.silu(group_norm(hidden, groups, total_rows)).astype(jnp.bfloat16)
    result = latents.astype(jnp.float32) + convolve(
        padded_field(second), second_conv_weight, rows, width
    )
    return result.astype(jnp.bfloat16)


def solution(mesh):
    in_specs = (
        P("req", "band", None, None),
        P("req", None),
        P("req", None),
        P(),
        P(),
        P(("band", "req"), None, None, None, None),
        P(("band", "req"), None, None),
        P(),
        P(),
    )
    out_specs = P("req", "band", None, None)
    return jax.shard_map(shards, mesh=mesh, in_specs=in_specs, out_specs=out_specs, check_vma=False)
```

profile of v0, /device:TPU:1, one launch (start us, length us, event | category | flops | bytes accessed | tf_op | source)
XLA Modules:
  0.0 247.0 jit_solution(5769340079304339442)
XLA Ops:
  7.3 1.6 convert_reduce_fusion
  9.1 12.6 %psum.42 = f32[1,32]{1,0:T(1,128)S(1)} all-reduce(f32[1,32]{1,0:T(1,128)S(1)} %bitcast.261), channel_id=1, replica_groups=mesh['band'=8,'req'=4] {'band'}, use_global_device_ids=true, to_apply=%region_2.3 | all-reduce | flops 32 | bytes 256 | tf_op jit(solution)/shard_map/psum | solution.py:26
  22.6 14.2 %psum.43 = f32[1,32]{1,0:T(1,128)S(1)} all-reduce(f32[1,32]{1,0:T(1,128)S(1)} %bitcast.262), channel_id=1, replica_groups=mesh['band'=8,'req'=4] {'band'}, use_global_device_ids=true, to_apply=%region_5.6 | all-reduce | flops 32 | bytes 256 | tf_op jit(solution)/shard_map/psum | solution.py:29
  38.0 1.9 collective-permute-start
  40.0 2.4 collective-permute-start.1
  43.0 12.7 %all_gather.7 = bf16[4,64,320]{2,1,0:T(8,128)(2,1)S(1)} all-gather(bf16[1,64,320]{2,1,0:T(8,128)(2,1)S(1)} %copy-done.14), channel_id=1, replica_groups=mesh['band'=8,'req'=4] {'req'}, dimensions={0}, use_global_device_ids=true | all-gather | bytes 204800 | tf_op jit(solution)/shard_map/all_gather | solution.py:112
  57.2 24.0 %psum.45 = bf16[64,320]{1,0:T(8,128)(2,1)S(1)} all-reduce(bf16[64,320]{1,0:T(8,128)(2,1)S(1)} %select_reduce_fusion.1), channel_id=1, replica_groups=mesh['band'=8,'req'=4] {'band'}, use_global_device_ids=true, to_apply=%region_10.11 | all-reduce | flops 20480 | bytes 81920 | tf_op jit(solution)/shard_map/psum | solution.py:117
  81.6 3.3 %fusion.32 = f32[4,512,320]{1,2,0:T(8,128)} fusion(bf16[1,4,512,320]{2,3,1,0:T(8,128)(2,1)S(1)} %fusion.8, bf16[3,3,320,320]{3,2,1,0:T(8,128)(2,1)} %param.13), kind=kOutput, calls=%fused_computation.57 | convolution fusion | flops 419430400 | bytes 4177920 | tf_op jit(solution)/shard_map/qhwc,cd->qhwd/dot_general | solution.py:43
  85.6 3.2 %fusion.15 = bf16[1,6,514,320]{2,3,1,0:T(8,128)(2,1)S(1)} fusion(bf16[1,1,512,320]{2,3,1,0:T(8,128)(2,1)} %collective-permute-done.1, bf16[1,4,512,320]{2,3,1,0:T(8,128)(2,1)} %copy-done.2, bf16[1,1,512,320]{2,3,1,0:T(8,128)(2,1)} %copy-done.8), kind=kLoop, calls=%fused_computation.25 | loop fusion | flops 11842560 | bytes 3939840 | tf_op jit(solution)/shard_map/concatenate | solution.py:18
  88.9 2.4 fusion.56
  91.3 2.6 %fusion.54 = f32[4,512,320]{1,2,0:T(8,128)} fusion(bf16[1,6,514,320]{2,3,1,0:T(8,128)(2,1)S(1)} %fusion.15, bf16[3,3,320,320]{3,2,1,0:T(8,128)(2,1)S(1)} %copy-done.11), kind=kOutput, calls=%fused_computation.80 | convolution fusion | flops 419430400 | bytes 4177920 | tf_op jit(solution)/shard_map/qhwc,cd->qhwd/dot_general | solution.py:43
  93.8 2.4 fusion.52
  96.2 2.6 %fusion.51 = f32[4,512,320]{1,2,0:T(8,128)} fusion(bf16[1,6,514,320]{2,3,1,0:T(8,128)(2,1)S(1)} %fusion.15, bf16[3,3,320,320]{3,2,1,0:T(8,128)(2,1)S(1)} %copy-done.11), kind=kOutput, calls=%fused_computation.77 | convolution fusion | flops 419430400 | bytes 4177920 | tf_op jit(solution)/shard_map/qhwc,cd->qhwd/dot_general | solution.py:43
  98.8 2.4 fusion.49
  101.2 2.5 %fusion.47 = f32[4,512,320]{1,2,0:T(8,128)} fusion(bf16[1,6,514,320]{2,3,1,0:T(8,128)(2,1)S(1)} %fusion.15, bf16[3,3,320,320]{3,2,1,0:T(8,128)(2,1)S(1)} %copy-done.11), kind=kOutput, calls=%fused_computation.73 | convolution fusion | flops 419430400 | bytes 4177920 | tf_op jit(solution)/shard_map/qhwc,cd->qhwd/dot_general | solution.py:43
  103.7 2.3 fusion.41
  106.0 3.0 %select_reduce_fusion = bf16[3,3,320,64]{2,3,1,0:T(8,128)(2,1)} fusion(bf16[4,3,3,320,64]{3,4,2,1,0:T(8,128)(2,1)} %all-gather.2.cloned.1.call-done, pred[4]{0:T(512)(128)(4,1)S(1)} %add_compare_fusion), kind=kLoop, calls=%fused_computation.26 | loop fusion | flops 1290240 | bytes 1843204 | tf_op jit(solution)/shard_map/reduce_sum | solution.py:73
  109.0 3.7 %fusion.60 = f32[4,512,320]{1,2,0:T(8,128)} fusion(bf16[1,1,512,320]{2,3,1,0:T(8,128)(2,1)} %collective-permute-done.1, bf16[1,4,512,320]{2,3,1,0:T(8,128)(2,1)} %copy-done.2, bf16[3,3,320,320]{3,2,1,0:T(8,128)(2,1)} %param.13), kind=kOutput, calls=%fused_computation.85 | convolution fusion | flops 422051840 | bytes 4505600 | tf_op jit(solution)/shard_map/qhwc,cd->qhwd/dot_general | solution.py:43
  112.7 51.3 %all-reduce.4.cloned.1.call-done = bf16[1,3,3,320,64]{3,4,2,1,0:T(8,128)(2,1)} async-done(((bf16[1,3,3,320,64]{3,4,2,1,0:T(8,128)(2,1)}), bf16[1,3,3,320,64]{3,4,2,1,0:T(8,128)(2,1)}) %all-reduce.4.cloned.1.call-update) | async-done | bytes 368656 | tf_op jit(solution)/shard_map/psum | solution.py:116
  164.1 1.8 fusion.34
  165.9 2.5 %fusion.62 = f32[4,512,64]{1,2,0:T(8,128)} fusion(bf16[1,1,512,320]{2,3,1,0:T(8,128)(2,1)} %collective-permute-done.1, bf16[1,4,512,320]{2,3,1,0:T(8,128)(2,1)} %copy-done.2, bf16[1,3,3,320,64]{3,4,2,1,0:T(8,128)(2,1)} %all-reduce.4.cloned.1.call-done), kind=kOutput, calls=%fused_computation.86 | convolution fusion | flops 86507520 | bytes 2211840 | tf_op jit(solution)/shard_map/qhwc,qcd->qhwd/dot_general | solution.py:57
  170.2 1.4 fusion.55
  172.7 13.4 %fusion.118 = (f32[320]{0:T(512)S(1)}, f32[4,512,320]{1,2,0:T(8,128)}) fusion(f32[320]{0:T(512)S(1)} %convolution_reduce_fusion, bf16[64,320]{1,0:T(8,128)(2,1)S(1)} %psum.45, f32[4,512,64]{1,2,0:T(8,128)} %fusion.55, f32[4,512,64]{1,2,0:T(8,128)} %fusion.62, f32[4,512,64]{1,2,0:T(8,128)S(1)} %fusion.53, f32[4,512,64]{1,2,0:T(8,128)} %fusion.46, ...), kind=kOutput, calls=%fused_computation.158 | convolution fusion | flops 175636160 | bytes 29723904 | tf_op jit(solution)/shard_map/qhwk,qkc->qhwc/dot_general | solution.py:133
  186.3 12.8 %psum.46 = f32[1,32]{1,0:T(1,128)S(1)} all-reduce(f32[1,32]{1,0:T(1,128)S(1)} %bitcast.263), channel_id=1, replica_groups=mesh['band'=8,'req'=4] {'band'}, use_global_device_ids=true, to_apply=%region_13.14 | all-reduce | flops 32 | bytes 256 | tf_op jit(solution)/shard_map/psum | solution.py:26
  199.3 2.2 multiply_reduce_fusion
  201.7 11.8 %psum.47 = f32[1,32]{1,0:T(1,128)S(1)} all-reduce(f32[1,32]{1,0:T(1,128)S(1)} %bitcast.260), channel_id=1, replica_groups=mesh['band'=8,'req'=4] {'band'}, use_global_device_ids=true, to_apply=%region_16.17 | all-reduce | flops 32 | bytes 256 | tf_op jit(solution)/shard_map/psum | solution.py:29
  214.7 1.9 collective-permute-start.2
  216.6 2.4 collective-permute-start.3
  219.1 2.8 %fusion.68 = f32[4,512,320]{1,2,0:T(8,128)} fusion(bf16[3,3,320,320]{3,2,1,0:T(8,128)(2,1)S(1)} %copy-done.12, f32[4,512,320]{1,2,0:T(8,128)S(1)} %copy-done.5, f32[320]{0:T(512)S(1)} %mul.85, f32[320]{0:T(512)S(1)} %sub.52), kind=kOutput, calls=%fused_computation.91 | convolution fusion | flops 424017920 | bytes 5492736 | tf_op jit(solution)/shard_map/qhwc,cd->qhwd/dot_general | solution.py:43
  221.9 5.0 %collective-permute-done.3 = bf16[1,1,512,320]{2,3,1,0:T(8,128)(2,1)S(1)} collective-permute-done((bf16[1,1,512,320]{2,3,1,0:T(8,128)(2,1)S(1)}, bf16[1,1,512,320]{2,3,1,0:T(8,128)(2,1)S(1)}, u32[]{:S(2)}, u32[]{:S(2)}) %collective-permute-start.3) | collective-permute-done | bytes 327712 | tf_op jit(solution)/shard_map/ppermute | solution.py:17
  226.9 1.7 select_maximum_fusion
  236.3 3.8 %fusion.10 = bf16[1,4,512,320]{2,3,1,0:T(8,128)(2,1)} fusion(bf16[1,4,512,320]{2,3,1,0:T(8,128)(2,1)S(1)} %copy-done.7, f32[4,512,320]{1,2,0:T(8,128)S(1)} %fusion.18, f32[4,512,320]{1,2,0:T(8,128)S(1)} %fusion.21, f32[4,512,320]{1,2,0:T(8,128)S(1)} %fusion.22, f32[4,512,320]{1,2,0:T(8,128)S(1)} %copy-done.10, f32[4,512,320]{1,2,0:T(8,128)S(1)} %fusion.23, ...), kind=kOutput, calls=%fused_computation.15 | convolution fusion | flops 426639360 | bytes 25149440 | tf_op jit(solution)/shard_map/qhwc,cd->qhwd/dot_general | solution.py:43
  (83 shorter events, 18.0 us)
Async XLA Ops:
  6.5 74.7 %copy-start = (bf16[1280,320]{0,1:T(8,128)(2,1)S(1)}, bf16[1280,320]{0,1:T(8,128)(2,1)}, u32[]{:S(2)}) copy-start(bf16[1280,320]{0,1:T(8,128)(2,1)} %param.17) | copy-start | bytes 2457604
  6.5 15.3 %copy-start.6 = (bf16[1,4,512,320]{2,3,1,0:T(8,128)(2,1)S(1)}, bf16[1,4,512,320]{2,3,1,0:T(8,128)(2,1)}, u32[]{:S(2)}) copy-start(bf16[1,4,512,320]{2,3,1,0:T(8,128)(2,1)} %param.9) | copy-start | bytes 3932164
  6.5 99.5 %all-gather.2.cloned.1.call-start = ((), (), s32[]{:S(2)}) async-start(), calls=%async_computation | async-start | bytes 2211840 | tf_op jit(solution)/shard_map/all_gather | solution.py:111
  7.3 156.8 %all-reduce.4.cloned.1.call-start = ((), (), s32[]{:S(2)}) async-start(), calls=%async_computation.1 | async-start | bytes 884736 | tf_op jit(solution)/shard_map/psum | solution.py:116
  21.9 21.1 %copy-start.14 = (bf16[1,64,320]{2,1,0:T(8,128)(2,1)S(1)}, bf16[1,64,320]{2,1,0:T(8,128)(2,1)}, u32[]{:S(2)}) copy-start(bf16[1,64,320]{2,1,0:T(8,128)(2,1)} %param.15) | copy-start | bytes 122884
  22.4 33.3 %copy-start.16 = (s32[32]{0:T(128)S(1)}, s32[32]{0:T(128)}, u32[]{:S(2)}) copy-start(s32[32]{0:T(128)} %param.12) | copy-start | bytes 388
  22.4 58.8 %copy-start.15 = (bf16[1,1280]{1,0:T(2,128)(2,1)S(1)}, bf16[1,1280]{1,0:T(2,128)(2,1)}, u32[]{:S(2)}) copy-start(bf16[1,1280]{1,0:T(2,128)(2,1)} %param.10) | copy-start | bytes 7684
  38.0 46.9 %copy-start.2 = (bf16[1,4,512,320]{2,3,1,0:T(8,128)(2,1)}, bf16[1,4,512,320]{2,3,1,0:T(8,128)(2,1)S(1)}, u32[]{:S(2)}) copy-start(bf16[1,4,512,320]{2,3,1,0:T(8,128)(2,1)S(1)} %fusion.8) | copy-start | bytes 3932164
  38.0 46.9 %collective-permute-start = (bf16[1,1,512,320]{2,3,1,0:T(8,128)(2,1)S(1)}, bf16[1,1,512,320]{2,3,1,0:T(8,128)(2,1)S(1)}, u32[]{:S(2)}, u32[]{:S(2)}) collective-permute-start(bf16[1,1,512,320]{2,3,1,0:T(8,128)(2,1)S(1)} %get-tuple-element.7), channel_id=1, source_target_pairs={{0,4},{4,8},{8,12},{12,16},{16,20},{20,24},{24,28},{1,5},{5,9},{9,... | collective-permute-start | bytes 983048 | tf_op jit(solution)/shard_map/ppermute | solution.py:16
  40.0 45.7 %collective-permute-start.1 = (bf16[1,1,512,320]{2,3,1,0:T(8,128)(2,1)S(1)}, bf16[1,1,512,320]{2,3,1,0:T(8,128)(2,1)}, u32[]{:S(2)}, u32[]{:S(2)}) collective-permute-start(bf16[1,1,512,320]{2,3,1,0:T(8,128)(2,1)S(1)} %get-tuple-element.8), channel_id=1, source_target_pairs={{4,0},{8,4},{12,8},{16,12},{20,16},{24,20},{28,24},{5,1},{9,5},{13... | collective-permute-start | bytes 983048 | tf_op jit(solution)/shard_map/ppermute | solution.py:17
  84.9 4.0 %copy-start.11 = (bf16[3,3,320,320]{3,2,1,0:T(8,128)(2,1)S(1)}, bf16[3,3,320,320]{3,2,1,0:T(8,128)(2,1)}, u32[]{:S(2)}) copy-start(bf16[3,3,320,320]{3,2,1,0:T(8,128)(2,1)} %param.13) | copy-start | bytes 5529604
  84.9 0.7 copy-start.8
  85.6 3.2 %copy-start.3 = (bf16[1,4,512,320]{2,3,1,0:T(8,128)(2,1)S(1)}, bf16[1,4,512,320]{2,3,1,0:T(8,128)(2,1)}, u32[]{:S(2)}) copy-start(bf16[1,4,512,320]{2,3,1,0:T(8,128)(2,1)} %copy-done.2) | copy-start | bytes 3932164
  85.6 3.2 %copy-start.9 = (bf16[1,1,512,320]{2,3,1,0:T(8,128)(2,1)S(1)}, bf16[1,1,512,320]{2,3,1,0:T(8,128)(2,1)}, u32[]{:S(2)}) copy-start(bf16[1,1,512,320]{2,3,1,0:T(8,128)(2,1)} %copy-done.8) | copy-start | bytes 983044
  164.1 4.4 %copy-start.4 = (bf16[1,4,512,320]{2,3,1,0:T(8,128)(2,1)S(1)}, bf16[1,4,512,320]{2,3,1,0:T(8,128)(2,1)}, u32[]{:S(2)}) copy-start(bf16[1,4,512,320]{2,3,1,0:T(8,128)(2,1)} %copy-done.2) | copy-start | bytes 3932164
  164.1 4.4 %copy-start.13 = (bf16[1,3,3,320,64]{3,4,2,1,0:T(8,128)(2,1)S(1)}, bf16[1,3,3,320,64]{3,4,2,1,0:T(8,128)(2,1)}, u32[]{:S(2)}) copy-start(bf16[1,3,3,320,64]{3,4,2,1,0:T(8,128)(2,1)} %all-reduce.4.cloned.1.call-done) | copy-start | bytes 1105924
  186.1 27.6 %copy-start.5 = (f32[4,512,320]{1,2,0:T(8,128)S(1)}, f32[4,512,320]{1,2,0:T(8,128)}, u32[]{:S(2)}) copy-start(f32[4,512,320]{1,2,0:T(8,128)} %get-tuple-element.10) | copy-start | bytes 7864324
  213.7 5.4 %copy-start.12 = (bf16[3,3,320,320]{3,2,1,0:T(8,128)(2,1)S(1)}, bf16[3,3,320,320]{3,2,1,0:T(8,128)(2,1)}, u32[]{:S(2)}) copy-start(bf16[3,3,320,320]{3,2,1,0:T(8,128)(2,1)} %param.16) | copy-start | bytes 5529604
  214.7 7.2 %collective-permute-start.2 = (bf16[1,1,512,320]{2,3,1,0:T(8,128)(2,1)S(1)}, bf16[1,1,512,320]{2,3,1,0:T(8,128)(2,1)S(1)}, u32[]{:S(2)}, u32[]{:S(2)}) collective-permute-start(bf16[1,1,512,320]{2,3,1,0:T(8,128)(2,1)S(1)} %get-tuple-element.5), channel_id=1, source_target_pairs={{0,4},{4,8},{8,12},{12,16},{16,20},{20,24},{24,28},{1,5},{5,9},{9,... | collective-permute-start | bytes 983048 | tf_op jit(solution)/shard_map/ppermute | solution.py:16
  216.6 10.2 %collective-permute-start.3 = (bf16[1,1,512,320]{2,3,1,0:T(8,128)(2,1)S(1)}, bf16[1,1,512,320]{2,3,1,0:T(8,128)(2,1)S(1)}, u32[]{:S(2)}, u32[]{:S(2)}) collective-permute-start(bf16[1,1,512,320]{2,3,1,0:T(8,128)(2,1)S(1)} %get-tuple-element.6), channel_id=1, source_target_pairs={{4,0},{8,4},{12,8},{16,12},{20,16},{24,20},{28,24},{5,1},{9,5},{13... | collective-permute-start | bytes 983048 | tf_op jit(solution)/shard_map/ppermute | solution.py:17
  234.2 1.3 copy-start.7
  234.2 2.1 copy-start.10
  236.3 3.8 %copy-start.1 = (bf16[1280,320]{0,1:T(8,128)(2,1)S(1)}, bf16[1280,320]{0,1:T(8,128)(2,1)}, u32[]{:S(2)}) copy-start(bf16[1280,320]{0,1:T(8,128)(2,1)} %param.17) | copy-start | bytes 2457604
Sparse Core Ops, SparseCore 0:
  8.9 43.8 all-gather.1
  109.1 54.9 all-reduce.3
where the time goes:
time: 248 us; the launch traced here: 247 us
  blocking collectives  88 us (35%)
  matrix products  59.6 us (24%)
  waiting for transfers between devices  57.1 us (23%)
  other arithmetic  15.9 us (6%)
  between operations  14.4 us (6%)
  starting transfers between devices  8.73 us (4%)
  local copies, waits for them, and re-layouts  3.26 us (1%)
    psum x1, waiting for transfers between devices, shards(): lax.psum(part_down, 'band').astype(jnp.float32)  51.3 us
    dot_general x18, matrix products, convolve(): jnp.einsum('qhwc,cd->qhwd', padded[:, row_tap:row_tap + rows, col_tap:col...  37.3 us
    psum x2, blocking collectives, group_norm(): lax.psum(jnp.sum(deviation * deviation, axis=(1, 2, 4)), 'band') / count  26 us
    psum x2, blocking collectives, group_norm(): sums = lax.psum(jnp.sum(grouped, axis=(1, 2, 4)), 'band')  25.4 us
    psum x1, blocking collectives, shards(): lax.psum(part_up, 'band').astype(jnp.float32)  24 us
    dot_general x1, matrix products, shards(): jnp.einsum('qhwk,qkc->qhwc', lowrank, chosen_up, preferred_element_type=j...  13.4 us
    all_gather x1, blocking collectives, shards(): lax.all_gather(stored_up_weight, 'req', axis=0, tiled=True)  12.7 us
    dot_general x8, matrix products, convolve_each(): jnp.einsum('qhwc,qcd->qhwd', padded[:, row_tap:row_tap + rows, col_tap:co...  8.61 us
  transfers between devices with their start and end apart: 6, of which 2 were waited for; matrix products, arithmetic and copies ran while one was open for 15% of the time, Pallas kernels for 0%

commit v1 on v0

v1 whole, which is shorter than its diff:
```python
import functools

import jax
import jax.numpy as jnp
import numpy as np
from jax import lax
from jax.experimental import pallas as pl
from jax.experimental.pallas import tpu as pltpu
from jax.sharding import PartitionSpec as P

G = 32
EPS = 1e-05
MESH = pl.DeviceIdType.MESH
F32 = jnp.float32
BF16 = jnp.bfloat16
LANES = 128
CHUNK = 64


def round_up(value, step):
    return -(-value // step) * step


def split3(v):
    hi = v.astype(BF16)
    rest = v - hi.astype(F32)
    mid = rest.astype(BF16)
    return hi, mid, (rest - mid.astype(F32)).astype(BF16)


def kernel(
    dims,
    lat_ref, temb_ref, ra_ref, row_ref, w1_hbm, down_hbm, up_hbm, w2_hbm, tp_hbm, gg_ref,
    out_ref,
    lat, act, x, hid, w1, w2, rhs2, up_pad, tp, down, up, shift,
    stat1, stat2, slots, packed, recv1, sel, recv2, full,
    hsend, hrecv, musend, murecv, outbuf,
    ld_sem, w1_sem, w2_sem, out_sem,
    s1s, s1r, s2s, s2r, sls, slr, p1s, p1r, p2s, p2r, p3s, p3r, has, har, hbs, hbr, hms, hmr,
):
    B, R, rows, width, C, rank, piece = dims
    CP = round_up(C, LANES)
    count = rows * width
    me = lax.axis_index("band")
    mr = lax.axis_index("req")
    half = 9 * C // 2

    def band(d):
        return lax.rem(me + d, B)

    def req(e):
        return lax.rem(mr + e, R)

    ld = [
        pltpu.make_async_copy(lat_ref.at[0], lat.at[pl.ds(1, rows)], ld_sem.at[0]),
        pltpu.make_async_copy(down_hbm.at[0], down, ld_sem.at[1]),
        pltpu.make_async_copy(up_hbm.at[0], up, ld_sem.at[2]),
        pltpu.make_async_copy(tp_hbm, tp, ld_sem.at[3]),
    ]
    for copy in ld:
        copy.start()

    def weight_copies(src, dst, sems):
        copies = []
        for i in range(3):
            for j in range(3):
                k = (i * 3 + j) * 2
                copies.append(pltpu.make_async_copy(
                    src.at[i, j, pl.ds(0, 256)], dst.at[i, pl.ds(256 * j, 256)], sems.at[k]))
                copies.append(pltpu.make_async_copy(
                    src.at[i, j, pl.ds(256, 64)], dst.at[i, pl.ds(768 + 64 * j, 64)], sems.at[k + 1]))
        return copies

    w1_copies = weight_copies(w1_hbm, w1, w1_sem)
    w2_copies = weight_copies(w2_hbm, w2, w2_sem)
    for copy in w1_copies + w2_copies:
        copy.start()

    barrier = pltpu.get_barrier_semaphore()
    for d in range(1, B):
        pl.semaphore_signal(barrier, inc=1, device_id={"band": band(d)}, device_id_type=MESH)
    for e in range(1, R):
        pl.semaphore_signal(barrier, inc=1, device_id={"req": req(e)}, device_id_type=MESH)

    slot = row_ref[ra_ref[0, 0]]
    slots[0] = jnp.full((8, LANES), slot, jnp.int32)
    ld[1].wait()
    ld[2].wait()
    flat = packed
    total_rows = half + 3 * rank
    zero64 = jnp.zeros((rank, 64), BF16)
    for start in range(0, half, 160):
        t0, c0 = start // C, start % C
        t1, c1 = (start + half) // C, (start + half) % C
        flat[pl.ds(start, 160), :] = jnp.concatenate(
            [down[t0 // 3, t0 % 3, pl.ds(c0, 160), :], down[t1 // 3, t1 % 3, pl.ds(c1, 160), :]], axis=1)
    flat[pl.ds(half, rank), :] = up[:, 0:128]
    flat[pl.ds(half + rank, rank), :] = up[:, 128:256]
    flat[pl.ds(half + 2 * rank, rank), :] = jnp.concatenate([up[:, 256:320], zero64], axis=1)
    pad_rows = B * piece - total_rows
    if pad_rows:
        flat[pl.ds(total_rows, pad_rows), :] = jnp.zeros((pad_rows, LANES), BF16)

    ld[0].wait()
    shift[...] = jnp.zeros_like(shift)
    stat1[0] = jnp.zeros((8, CP), F32)
    stat2[0] = jnp.zeros((8, CP), F32)

    def lat_sum(k, acc):
        v = lat[1 + k // (width // CHUNK), pl.ds(pl.multiple_of((k % (width // CHUNK)) * CHUNK, CHUNK), CHUNK), :].astype(F32)
        return acc + jnp.sum(v.reshape(CHUNK // 8, 8, C), axis=0)

    steps = rows * (width // CHUNK)
    sums = lax.fori_loop(0, steps, lat_sum, jnp.zeros((8, C), F32))
    mean = jnp.sum(sums, axis=0, keepdims=True) * (1.0 / count)

    def lat_dev(k, acc):
        v = lat[1 + k // (width // CHUNK), pl.ds(pl.multiple_of((k % (width // CHUNK)) * CHUNK, CHUNK), CHUNK), :].astype(F32)
        v = v - mean
        return acc + jnp.sum((v * v).reshape(CHUNK // 8, 8, C), axis=0)

    devs = lax.fori_loop(0, steps, lat_dev, jnp.zeros((8, C), F32))
    stat1[0, 0:1, 0:C] = mean
    stat1[0, 1:2, 0:C] = jnp.sum(devs, axis=0, keepdims=True)

    pl.semaphore_wait(barrier, B - 1 + R - 1)

    def send_stats(buf, ss, rs):
        out = []
        for d in range(1, B):
            out.append(pltpu.make_async_remote_copy(
                src_ref=buf.at[0], dst_ref=buf.at[d], send_sem=ss.at[d], recv_sem=rs.at[d],
                device_id={"band": band(d)}, device_id_type=MESH))
            out[-1].start()
        return out

    stat1_copies = send_stats(stat1, s1s, s1r)
    slot_copies = []
    for e in range(1, R):
        slot_copies.append(pltpu.make_async_remote_copy(
            src_ref=slots.at[0], dst_ref=slots.at[e], send_sem=sls.at[e], recv_sem=slr.at[e],
            device_id={"req": req(e)}, device_id_type=MESH))
        slot_copies[-1].start()

    p1_copies = []
    for d in range(1, B):
        p1_copies.append(pltpu.make_async_remote_copy(
            src_ref=packed.at[pl.ds(pl.multiple_of(band(d) * piece, 16), piece)], dst_ref=recv1.at[d],
            send_sem=p1s.at[d], recv_sem=p1r.at[d], device_id={"band": band(d)}, device_id_type=MESH))
        p1_copies[-1].start()

    def up_copy():
        return pltpu.make_async_remote_copy(
            src_ref=lat.at[1], dst_ref=lat.at[rows + 1], send_sem=has.at[0], recv_sem=har.at[0],
            device_id={"band": lax.rem(me + B - 1, B)}, device_id_type=MESH)

    def down_copy():
        return pltpu.make_async_remote_copy(
            src_ref=lat.at[rows], dst_ref=lat.at[0], send_sem=has.at[1], recv_sem=har.at[1],
            device_id={"band": band(1)}, device_id_type=MESH)

    @pl.when(me > 0)
    def _():
        up_copy().start()

    @pl.when(me < B - 1)
    def _():
        down_copy().start()

    ld[3].wait()
    t = temb_ref[...].astype(F32)
    t = (t / (1.0 + jnp.exp(-t))).astype(BF16).astype(F32)
    t = jnp.broadcast_to(t, (16, t.shape[1])).astype(BF16)
    shift[0:1, 0:C] = jnp.dot(t, tp[...], preferred_element_type=F32)[0:1]

    act[...] = jnp.zeros_like(act)
    for i in range(3):
        w1[i, pl.ds(960, 64), :] = jnp.zeros((64, C), BF16)
        w2[i, pl.ds(960, 64), :] = jnp.zeros((64, C), BF16)
        rhs2[i, pl.ds(960, 64), :] = jnp.zeros((64, LANES), BF16)

    def group_sum(v):
        v = jnp.broadcast_to(v, (16, CP))
        gg = gg_ref[...]
        return sum(jnp.dot(part, gg, preferred_element_type=F32) for part in split3(v))[0:1]

    def combine(buf):
        cpg = C // G
        total = buf[0]
        for d in range(1, B):
            total = total + buf[d]
        m = group_sum(total[0:1]) * (1.0 / (cpg * B))
        dev = jnp.zeros((1, CP), F32)
        for d in range(B):
            diff = buf[d][0:1] - m
            dev = dev + diff * diff
        valid = lax.broadcasted_iota(jnp.int32, (1, CP), 1) < C
        dev = jnp.where(valid, total[1:2] + float(count) * dev, 0.0)
        spread = group_sum(dev) * (1.0 / (float(count) * cpg * B))
        return m, 0.5 * lax.rsqrt(spread + EPS)

    def silu_half(h):
        return h * jnp.tanh(h) + h

    def spread_row(r):
        for c in range(0, width, CHUNK):
            v = act[pl.ds(c, CHUNK + 16), :]
            before = pltpu.roll(v, 1, 0)[8:8 + CHUNK]
            after = pltpu.roll(v, CHUNK + 15, 0)[8:8 + CHUNK]
            here = v[8:8 + CHUNK]
            x[r, pl.ds(c, CHUNK), 0:256] = before[:, 0:256].astype(BF16)
            x[r, pl.ds(c, CHUNK), 256:512] = here[:, 0:256].astype(BF16)
            x[r, pl.ds(c, CHUNK), 512:768] = after[:, 0:256].astype(BF16)
            x[r, pl.ds(c, CHUNK), 768:896] = (before[:, 256:384] + pltpu.roll(here[:, 256:384], 64, 1)).astype(BF16)
            x[r, pl.ds(c, CHUNK), 896:1024] = after[:, 256:384].astype(BF16)

    for copy in stat1_copies:
        copy.wait_recv()
    m1, a1 = combine(stat1)
    m1, a1 = m1[:, 0:C], a1[:, 0:C]

    def first_row(r):
        for c in range(0, width, CHUNK):
            v = lat[r, pl.ds(c, CHUNK), :].astype(F32)
            act[pl.ds(8 + c, CHUNK), 0:C] = silu_half((v - m1) * a1)
        spread_row(r)

    def first_body(k, _):
        first_row(1 + k)
        return 0

    lax.fori_loop(0, rows, first_body, 0)

    for copy in p1_copies + slot_copies:
        copy.wait_recv()
    p2_copies = []
    own = packed[pl.ds(pl.multiple_of(me * piece, 16), piece), :].astype(F32)
    for n in range(R):
        e = (n + 1) % R
        wanted = slots[(R - e) % R][0:1]
        acc = own * (wanted == me * R + mr).astype(F32)
        for d in range(1, B):
            ident = lax.rem(me - d + B, B) * R + mr
            acc = acc + recv1[d].astype(F32) * (wanted == ident).astype(F32)
        sel[e] = acc.astype(BF16)
        if e:
            p2_copies.append(pltpu.make_async_remote_copy(
                src_ref=sel.at[e], dst_ref=recv2.at[e], send_sem=p2s.at[e], recv_sem=p2r.at[e],
                device_id={"req": req(e)}, device_id_type=MESH))
            p2_copies[-1].start()

    zero_row = jnp.zeros((width, 1024), BF16)

    @pl.when(me > 0)
    def _():
        down_copy().wait_recv()
        first_row(0)

    @pl.when(me == 0)
    def _():
        x[0] = zero_row

    @pl.when(me < B - 1)
    def _():
        up_copy().wait_recv()
        first_row(rows + 1)

    @pl.when(me == B - 1)
    def _():
        x[rows + 1] = zero_row

    for copy in w1_copies:
        copy.wait()

    def conv(r, weights, lo, hi):
        total = None
        for i in range(3):
            term = jnp.dot(x[r + i], weights[i, :, lo:hi], preferred_element_type=F32)
            total = term if total is None else total + term
        return total

    def main_body(r, _):
        hid[r, :, 0:256] = conv(r, w1, 0, 256) + shift[0:1, 0:256]
        return 0

    lax.fori_loop(0, 1, main_body, 0)

    for copy in p2_copies:
        copy.wait_recv()
    acc = sel[0].astype(F32)
    for e in range(1, R):
        acc = acc + recv2[e].astype(F32)
    full[me] = acc.astype(BF16)
    p3_copies = []
    for d in range(1, B):
        p3_copies.append(pltpu.make_async_remote_copy(
            src_ref=full.at[me], dst_ref=full.at[me], send_sem=p3s.at[d], recv_sem=p3r.at[d],
            device_id={"band": band(d)}, device_id_type=MESH))
        p3_copies[-1].start()

    lax.fori_loop(1, rows, main_body, 0)

    for d in range(1, B):
        pltpu.make_async_remote_copy(
            src_ref=full.at[me], dst_ref=full.at[lax.rem(me - d + B, B)], send_sem=p3s.at[d], recv_sem=p3r.at[d],
            device_id={"band": band(d)}, device_id_type=MESH).wait_recv()

    low_lane = lax.broadcasted_iota(jnp.int32, (1, LANES), 1) < 64

    def adapter_rows(start, size):
        parts = []
        while size:
            p, o = start // piece, start % piece
            take = min(size, piece - o)
            parts.append(full[p, pl.ds(o, take), :].astype(F32))
            start, size = start + take, size - take
        return parts[0] if len(parts) == 1 else jnp.concatenate(parts, axis=0)

    def place(i, k, start, size):
        main3 = w1[i, pl.ds(k, size), 256:320].astype(F32)
        main3 = jnp.concatenate([main3, jnp.zeros((size, 64), F32)], axis=1)
        if start < half:
            v = pltpu.roll(adapter_rows(start, size), 64, 1)
        else:
            v = adapter_rows(start - half, size)
        rhs2[i, pl.ds(k, size), :] = jnp.where(low_lane, main3, v).astype(BF16)

    for i in range(3):
        for j in range(3):
            base = (i * 3 + j) * C
            for c in range(0, C, 32):
                k = 256 * j + c if c < 256 else 768 + 64 * j + c - 256
                place(i, k, base + c, 32)
    up_pad[pl.ds(0, 64), :] = jnp.zeros((64, CP), BF16)
    for b in range(3):
        up_pad[pl.ds(64, rank), 128 * b:128 * b + 128] = adapter_rows(half + b * rank, rank).astype(BF16)

    def hidden_row(r):
        t = conv(r, rhs2, 0, 128)
        lifted = jnp.dot(t.astype(BF16), up_pad[...], preferred_element_type=F32)
        hid[r, :, 0:256] = hid[r, :, 0:256] + lifted[:, 0:256]
        hid[r, :, 256:384] = jnp.where(low_lane, t, 0.0) + lifted[:, 256:384] + shift[0:1, 256:384]

    def row_chunk(r, c):
        return hid[r, pl.ds(c, CHUNK), :]

    def row_sum(r):
        acc = jnp.zeros((8, CP), F32)
        for c in range(0, width, CHUNK):
            acc = acc + jnp.sum(row_chunk(r, c).reshape(CHUNK // 8, 8, CP), axis=0)
        return jnp.sum(acc, axis=0, keepdims=True)

    def edge_body(k, acc):
        r = k * (rows - 1)
        hidden_row(r)
        total = row_sum(r)
        mu = total * (1.0 / width)
        musend[k] = jnp.broadcast_to(mu, (8, CP))
        for c in range(0, width, CHUNK):
            hsend[k, pl.ds(c, CHUNK), :] = (row_chunk(r, c) - mu).astype(BF16)
        return acc + total

    def halo_copies(k):
        target = lax.rem(me + B - 1, B) if k == 0 else band(1)
        return (
            pltpu.make_async_remote_copy(
                src_ref=hsend.at[k], dst_ref=hrecv.at[1 - k], send_sem=hbs.at[k], recv_sem=hbr.at[k],
                device_id={"band": target}, device_id_type=MESH),
            pltpu.make_async_remote_copy(
                src_ref=musend.at[k], dst_ref=murecv.at[1 - k], send_sem=hms.at[k], recv_sem=hmr.at[k],
                device_id={"band": target}, device_id_type=MESH),
        )

    total = lax.fori_loop(0, 2, edge_body, jnp.zeros((1, CP), F32))

    @pl.when(me > 0)
    def _():
        for copy in halo_copies(0):
            copy.start()

    @pl.when(me < B - 1)
    def _():
        for copy in halo_copies(1):
            copy.start()

    def inner_body(r, acc):
        hidden_row(r)
        return acc + row_sum(r)

    total = lax.fori_loop(1, rows - 1, inner_body, total)
    mean2 = total * (1.0 / count)

    def dev_body(r, acc):
        for c in range(0, width, CHUNK):
            v = row_chunk(r, c) - mean2
            acc = acc + jnp.sum((v * v).reshape(CHUNK // 8, 8, CP), axis=0)
        return acc

    devs2 = lax.fori_loop(0, rows, dev_body, jnp.zeros((8, CP), F32))
    stat2[0, 0:1, :] = mean2
    stat2[0, 1:2, :] = jnp.sum(devs2, axis=0, keepdims=True)
    stat2_copies = send_stats(stat2, s2s, s2r)
    for copy in w2_copies:
        copy.wait()
    for copy in stat2_copies:
        copy.wait_recv()
    m2, a2 = combine(stat2)

    def second_body(r, _):
        for c in range(0, width, CHUNK):
            act[pl.ds(8 + c, CHUNK), :] = silu_half((row_chunk(r, c) - m2) * a2)
        spread_row(r + 1)
        return 0

    lax.fori_loop(0, rows, second_body, 0)

    def out_copy(r):
        return pltpu.make_async_copy(outbuf.at[r], out_ref.at[0, r], out_sem.at[r])

    def final_row(r):
        outbuf[r] = (lat[1 + r].astype(F32) + conv(r, w2, 0, C)).astype(BF16)

    def final_inner(r, _):
        final_row(r)
        out_copy(r).start()
        return 0

    lax.fori_loop(1, rows - 1, final_inner, 0)

    def halo_row(k, r):
        off = murecv[k][0:1] - m2
        for c in range(0, width, CHUNK):
            v = hrecv[k, pl.ds(c, CHUNK), :].astype(F32)
            act[pl.ds(8 + c, CHUNK), :] = silu_half((v + off) * a2)
        spread_row(r)

    @pl.when(me > 0)
    def _():
        for copy in halo_copies(1):
            copy.wait_recv()
        halo_row(0, 0)

    @pl.when(me < B - 1)
    def _():
        for copy in halo_copies(0):
            copy.wait_recv()
        halo_row(1, rows + 1)

    def final_edge(k, _):
        r = k * (rows - 1)
        final_row(r)
        out_copy(r).start()
        return 0

    lax.fori_loop(0, 2, final_edge, 0)

    for copy in stat1_copies + slot_copies + p1_copies + p2_copies + p3_copies + stat2_copies:
        copy.wait_send()

    @pl.when(me > 0)
    def _():
        up_copy().wait_send()
        for copy in halo_copies(0):
            copy.wait_send()

    @pl.when(me < B - 1)
    def _():
        down_copy().wait_send()
        for copy in halo_copies(1):
            copy.wait_send()

    for r in range(rows):
        out_copy(r).wait()


def block(mesh_shape, lat, temb, ra, stored_row, w1, down, up, w2, tp):
    B, R = mesh_shape["band"], mesh_shape["req"]
    _, rows, width, C = lat.shape
    rank = up.shape[1]
    CP = round_up(C, LANES)
    piece = round_up(-(-(9 * C // 2 + 3 * rank) // B), 16)
    dims = (B, R, rows, width, C, rank, piece)
    ids = np.arange(CP) // (C // G)
    ok = np.arange(CP) < C
    gg = jnp.asarray((ids[:, None] == ids[None, :]) & ok[:, None] & ok[None, :], dtype=BF16)
    hbm = pl.BlockSpec(memory_space=pl.ANY)
    vmem = pl.BlockSpec(memory_space=pltpu.VMEM)
    smem = pl.BlockSpec(memory_space=pltpu.SMEM)
    V = pltpu.VMEM
    dma = lambda n: pltpu.SemaphoreType.DMA((n,))
    scratch = [
        V((rows + 2, width, C), BF16), V((width + 16, CP), F32), V((rows + 2, width, 1024), BF16),
        V((rows, width, CP), F32), V((3, 1024, C), BF16), V((3, 1024, C), BF16), V((3, 1024, LANES), BF16),
        V((64 + rank, CP), BF16), V(tp.shape, BF16), V(down.shape[1:], BF16), V(up.shape[1:], BF16), V((8, CP), F32),
        V((B, 8, CP), F32), V((B, 8, CP), F32), V((R, 8, LANES), jnp.int32), V((B * piece, LANES), BF16),
        V((B, piece, LANES), BF16), V((R, piece, LANES), BF16), V((R, piece, LANES), BF16), V((B, piece, LANES), BF16),
        V((2, width, CP), BF16), V((2, width, CP), BF16), V((2, 8, CP), F32), V((2, 8, CP), F32), V((rows, width, C), BF16),
        dma(4), dma(18), dma(18), dma(rows),
        dma(B), dma(B), dma(B), dma(B), dma(R), dma(R), dma(B), dma(B), dma(R), dma(R), dma(B), dma(B),
        dma(2), dma(2), dma(2), dma(2), dma(2), dma(2),
    ]
    return pl.pallas_call(
        functools.partial(kernel, dims),
        out_shape=jax.ShapeDtypeStruct(lat.shape, BF16),
        in_specs=[hbm, vmem, smem, smem, hbm, hbm, hbm, hbm, hbm, vmem],
        out_specs=hbm,
        scratch_shapes=scratch,
        compiler_params=pltpu.CompilerParams(
            collective_id=0, has_side_effects=True, vmem_limit_bytes=48 * 1024 * 1024),
        name="block",
    )(lat, temb, ra, stored_row, w1, down, up, w2, tp, gg)


def solution(mesh):
    in_specs = (
        P("req", "band", None, None),
        P("req", None),
        P("req", None),
        P(),
        P(),
        P(("band", "req"), None, None, None, None),
        P(("band", "req"), None, None),
        P(),
        P(),
    )
    return jax.shard_map(
        functools.partial(block, dict(mesh.shape)), mesh=mesh, in_specs=in_specs,
        out_specs=P("req", "band", None, None), check_vma=False)
```

time: 248 us -> 63.9 us (0.26)
  blocking collectives: 88 us -> 0 us
  matrix products: 59.6 us -> 0 us
  waiting for transfers between devices: 57.1 us -> 0 us
  Pallas kernels: 0 us -> 54.5 us
  other arithmetic: 15.9 us -> 0 us
  between operations: 14.4 us -> 0.85 us
  starting transfers between devices: 8.73 us -> 0 us
  local copies, waits for them, and re-layouts: 3.26 us -> 8.26 us
    psum x5 -> x0, blocking collectives: 75.3 us -> none  [the longest x2 26 us: group_norm(): lax.psum(jnp.sum(deviation * deviation, axis=(1, 2, 4)), 'band') / count]
    dot_general x28 -> x0, matrix products: 59.6 us -> none  [the longest x18 37.3 us: convolve(): jnp.einsum('qhwc,cd->qhwd', padded[:, row_tap:row_tap + rows, col_tap:col...]
    pallas_call x0 -> x1, Pallas kernels: none -> 54.5 us  [block(): pl.pallas_call(functools.partial(kernel, dims), out_shape=jax.ShapeDtypeS...]
    psum x1 -> x0, waiting for transfers between devices: 51.3 us -> none  [shards(): lax.psum(part_down, 'band').astype(jnp.float32)]
    all_gather x1 -> x0, blocking collectives: 12.7 us -> none  [shards(): lax.all_gather(stored_up_weight, 'req', axis=0, tiled=True)]
    ppermute x4 -> x0, starting transfers between devices: 8.69 us -> none  [the longest x2 4.85 us: with_halo(): after = lax.ppermute(initial, axis, down)]
    reduce_sum x10 -> x0, other arithmetic: 8.47 us -> none  [the longest x1 2.97 us: select_rows(): jnp.sum(jnp.where(matches[:, :, None, None, None, None], down_piece[None]...]
    ppermute x4 -> x0, waiting for transfers between devices: 5.01 us -> none  [the longest x2 5.01 us: with_halo(): after = lax.ppermute(initial, axis, down)]
  transfers between devices with their start and end apart: 6 -> 0, of which waited for: 2 -> 0; matrix products, arithmetic and copies ran while one was open for 15% -> 0% of each run, Pallas kernels for 0% -> 0%
where the time goes in v1:
time: 63.9 us; the launch traced here: 63.6 us
  Pallas kernels  54.5 us (85%)
  local copies, waits for them, and re-layouts  8.26 us (13%)
  between operations  0.85 us (1%)
    pallas_call x1, Pallas kernels, block(): pl.pallas_call(functools.partial(kernel, dims), out_shape=jax.ShapeDtypeS...  54.5 us
    unnamed x19, local copies, waits for them, and re-layouts  6.71 us
    pallas_call x1, local copies, waits for them, and re-layouts, block(): pl.pallas_call(functools.partial(kernel, dims), out_shape=jax.ShapeDtypeS...  1.55 us

profile of v1, /device:TPU:1, one launch (start us, length us, event | category | flops | bytes accessed | tf_op | source)
XLA Modules:
  0.0 63.6 jit_solution(9283298962719706772)
XLA Ops:
  0.0 0.0 copy-start.7
  0.0 0.0 copy-start.6
  0.8 2.2 %copy.12.down_hbm = bf16[1,3,3,320,64]{4,3,2,1,0:T(8,128)(2,1)} copy(bf16[1,3,3,320,64]{3,4,2,1,0:T(8,128)(2,1)} %param.15) | data formatting | bytes 737280 | tf_op args[5]
  3.0 0.0 copy-done.7
  3.0 1.3 %copy.13.tp_hbm = bf16[1280,320]{1,0:T(8,128)(2,1)} copy(bf16[1280,320]{0,1:T(8,128)(2,1)S(1)} %copy-done.7) | data formatting | bytes 1638400 | tf_op args[8]
  4.3 0.0 copy-done.6
  4.3 0.0 copy-start.2
  4.3 0.0 copy-start.3
  4.3 0.0 copy-start.4
  4.3 0.0 copy-start.5
  4.3 0.9 %copy.11.lat_ref = bf16[1,4,512,320]{3,2,1,0:T(8,128)(2,1)S(1)} copy(bf16[1,4,512,320]{2,3,1,0:T(8,128)(2,1)S(1)} %copy-done.6) | data formatting | bytes 2621440 | tf_op args[0]
  5.1 0.1 copy-done.2
  5.2 0.0 copy-done.3
  5.2 0.0 copy-done.4
  5.2 0.0 copy-done.5
  5.2 0.0 copy-start
  5.2 1.2 %copy-done = bf16[1280,320]{1,0:T(8,128)(2,1)S(1)} copy-done((bf16[1280,320]{1,0:T(8,128)(2,1)S(1)}, bf16[1280,320]{1,0:T(8,128)(2,1)}, u32[]{:S(2)}) %copy-start) | copy-done | bytes 819224
  6.4 0.0 copy-start.1
  6.4 1.1 %copy-done.1 = bf16[1,3,3,320,64]{4,3,2,1,0:T(8,128)(2,1)S(1)} copy-done((bf16[1,3,3,320,64]{4,3,2,1,0:T(8,128)(2,1)S(1)}, bf16[1,3,3,320,64]{4,3,2,1,0:T(8,128)(2,1)}, u32[]{:S(2)}) %copy-start.1) | copy-done | bytes 368664
  7.5 54.5 %block.1 = bf16[1,4,512,320]{3,2,1,0:T(8,128)(2,1)S(1)} custom-call(bf16[1,4,512,320]{3,2,1,0:T(8,128)(2,1)S(1)} %copy.11.lat_ref, bf16[1,1280]{1,0:T(2,128)(2,1)S(1)} %copy-done.4, s32[1,1]{1,0:T(1,128)S(6)} %copy.15.ra_ref, s32[32]{0:T(128)S(1)} %copy-done.5, bf16[3,3,320,320]{3,2,1,0:T(8,128)(2,1)} %w1_hbm.1, bf16[1,3,3,320,64]{4,3,2,1,0:T(8,128)(2,1)S(1)} %copy-done.1, ...), custom_call_target="tpu_custom_call" | custom-call | tf_op jit(solution)/shard_map/block/pallas_call | solution.py:502
  62.1 1.6 %copy.14 = bf16[1,4,512,320]{2,3,1,0:T(8,128)(2,1)} copy(bf16[1,4,512,320]{3,2,1,0:T(8,128)(2,1)S(1)} %block.1) | data formatting | bytes 2621440 | tf_op jit(solution)/shard_map/block/pallas_call | solution.py:502
Async XLA Ops:
  0.0 3.0 %copy-start.7 = (bf16[1280,320]{0,1:T(8,128)(2,1)S(1)}, bf16[1280,320]{0,1:T(8,128)(2,1)}, u32[]{:S(2)}) copy-start(bf16[1280,320]{0,1:T(8,128)(2,1)} %param.18) | copy-start | bytes 2457604
  0.0 4.3 %copy-start.6 = (bf16[1,4,512,320]{2,3,1,0:T(8,128)(2,1)S(1)}, bf16[1,4,512,320]{2,3,1,0:T(8,128)(2,1)}, u32[]{:S(2)}) copy-start(bf16[1,4,512,320]{2,3,1,0:T(8,128)(2,1)} %param.10) | copy-start | bytes 3932164
  4.3 1.0 %copy-start.2 = (bf16[384,384]{1,0:T(8,128)(2,1)S(1)}, bf16[384,384]{1,0:T(8,128)(2,1)}, u32[]{:S(2)}) copy-start(bf16[384,384]{1,0:T(8,128)(2,1)} %constant.2.clone.gg_ref) | copy-start | bytes 884740
  4.3 1.0 %copy-start.3 = (bf16[1,64,320]{2,1,0:T(8,128)(2,1)S(1)}, bf16[1,64,320]{2,1,0:T(8,128)(2,1)}, u32[]{:S(2)}) copy-start(bf16[1,64,320]{2,1,0:T(8,128)(2,1)} %up_hbm.1) | copy-start | bytes 122884
  4.3 1.0 %copy-start.4 = (bf16[1,1280]{1,0:T(2,128)(2,1)S(1)}, bf16[1,1280]{1,0:T(2,128)(2,1)}, u32[]{:S(2)}) copy-start(bf16[1,1280]{1,0:T(2,128)(2,1)} %temb_ref.1) | copy-start | bytes 7684
  4.3 1.0 %copy-start.5 = (s32[32]{0:T(128)S(1)}, s32[32]{0:T(128)}, u32[]{:S(2)}) copy-start(s32[32]{0:T(128)} %row_ref.1) | copy-start | bytes 388
  5.2 1.2 %copy-start = (bf16[1280,320]{1,0:T(8,128)(2,1)S(1)}, bf16[1280,320]{1,0:T(8,128)(2,1)}, u32[]{:S(2)}) copy-start(bf16[1280,320]{1,0:T(8,128)(2,1)} %copy.13.tp_hbm) | copy-start | bytes 2457604
  6.4 1.1 %copy-start.1 = (bf16[1,3,3,320,64]{4,3,2,1,0:T(8,128)(2,1)S(1)}, bf16[1,3,3,320,64]{4,3,2,1,0:T(8,128)(2,1)}, u32[]{:S(2)}) copy-start(bf16[1,3,3,320,64]{4,3,2,1,0:T(8,128)(2,1)} %copy.12.down_hbm) | copy-start | bytes 1105924

commit v2 on v1

--- a/solution.py
+++ b/solution.py
@@ -89,11 +89,11 @@
     flat = packed
     total_rows = half + 3 * rank
     zero64 = jnp.zeros((rank, 64), BF16)
+    tap = [down[t // 3, t % 3].astype(F32).T.astype(BF16) for t in range(9)]
     for start in range(0, half, 160):
         t0, c0 = start // C, start % C
         t1, c1 = (start + half) // C, (start + half) % C
-        flat[pl.ds(start, 160), :] = jnp.concatenate(
-            [down[t0 // 3, t0 % 3, pl.ds(c0, 160), :], down[t1 // 3, t1 % 3, pl.ds(c1, 160), :]], axis=1)
+        flat[pl.ds(start, 160), :] = jnp.concatenate([tap[t0][c0:c0 + 160], tap[t1][c1:c1 + 160]], axis=1)
     flat[pl.ds(half, rank), :] = up[:, 0:128]
     flat[pl.ds(half + rank, rank), :] = up[:, 128:256]
     flat[pl.ds(half + 2 * rank, rank), :] = jnp.concatenate([up[:, 256:320], zero64], axis=1)
@@ -142,6 +142,24 @@
             device_id={"req": req(e)}, device_id_type=MESH))
         slot_copies[-1].start()
 
+    def up_copy():
+        return pltpu.make_async_remote_copy(
+            src_ref=lat.at[1], dst_ref=lat.at[rows + 1], send_sem=has.at[0], recv_sem=har.at[0],
+            device_id={"band": lax.rem(me + B - 1, B)}, device_id_type=MESH)
+
+    def down_copy():
+        return pltpu.make_async_remote_copy(
+            src_ref=lat.at[rows], dst_ref=lat.at[0], send_sem=has.at[1], recv_sem=har.at[1],
+            device_id={"band": band(1)}, device_id_type=MESH)
+
+    @pl.when(me > 0)
+    def _():
+        up_copy().start()
+
+    @pl.when(me < B - 1)
+    def _():
+        down_copy().start()
+
     p1_copies = []
     for d in range(1, B):
         p1_copies.append(pltpu.make_async_remote_copy(
@@ -149,29 +167,12 @@
             send_sem=p1s.at[d], recv_sem=p1r.at[d], device_id={"band": band(d)}, device_id_type=MESH))
         p1_copies[-1].start()
 
-    def up_copy():
-        return pltpu.make_async_remote_copy(
-            src_ref=lat.at[1], dst_ref=lat.at[rows + 1], send_sem=has.at[0], recv_sem=har.at[0],
-            device_id={"band": lax.rem(me + B - 1, B)}, device_id_type=MESH)
-
-    def down_copy():
-        return pltpu.make_async_remote_copy(
-            src_ref=lat.at[rows], dst_ref=lat.at[0], send_sem=has.at[1], recv_sem=har.at[1],
-            device_id={"band": band(1)}, device_id_type=MESH)
-
-    @pl.when(me > 0)
-    def _():
-        up_copy().start()
-
-    @pl.when(me < B - 1)
-    def _():
-        down_copy().start()
-
     ld[3].wait()
     t = temb_ref[...].astype(F32)
     t = (t / (1.0 + jnp.exp(-t))).astype(BF16).astype(F32)
     t = jnp.broadcast_to(t, (16, t.shape[1])).astype(BF16)
-    shift[0:1, 0:C] = jnp.dot(t, tp[...], preferred_element_type=F32)[0:1]
+    shift[0:1, 0:C] = lax.dot_general(
+        t, tp[...], (((1,), (1,)), ((), ())), preferred_element_type=F32)[0:1]
 
     act[...] = jnp.zeros_like(act)
     for i in range(3):
@@ -249,26 +250,6 @@
                 device_id={"req": req(e)}, device_id_type=MESH))
             p2_copies[-1].start()
 
-    zero_row = jnp.zeros((width, 1024), BF16)
-
-    @pl.when(me > 0)
-    def _():
-        down_copy().wait_recv()
-        first_row(0)
-
-    @pl.when(me == 0)
-    def _():
-        x[0] = zero_row
-
-    @pl.when(me < B - 1)
-    def _():
-        up_copy().wait_recv()
-        first_row(rows + 1)
-
-    @pl.when(me == B - 1)
-    def _():
-        x[rows + 1] = zero_row
-
     for copy in w1_copies:
         copy.wait()
 
@@ -283,7 +264,7 @@
         hid[r, :, 0:256] = conv(r, w1, 0, 256) + shift[0:1, 0:256]
         return 0
 
-    lax.fori_loop(0, 1, main_body, 0)
+    lax.fori_loop(1, rows - 1, main_body, 0)
 
     for copy in p2_copies:
         copy.wait_recv()
@@ -298,7 +279,27 @@
             device_id={"band": band(d)}, device_id_type=MESH))
         p3_copies[-1].start()
 
-    lax.fori_loop(1, rows, main_body, 0)
+    zero_row = jnp.zeros((width, 1024), BF16)
+
+    @pl.when(me > 0)
+    def _():
+        down_copy().wait_recv()
+        first_row(0)
+
+    @pl.when(me == 0)
+    def _():
+        x[0] = zero_row
+
+    @pl.when(me < B - 1)
+    def _():
+        up_copy().wait_recv()
+        first_row(rows + 1)
+
+    @pl.when(me == B - 1)
+    def _():
+        x[rows + 1] = zero_row
+
+    lax.fori_loop(0, 2, lambda k, c: main_body(k * (rows - 1), c), 0)
 
     for d in range(1, B):
         pltpu.make_async_remote_copy(
@@ -477,6 +478,8 @@
     B, R = mesh_shape["band"], mesh_shape["req"]
     _, rows, width, C = lat.shape
     rank = up.shape[1]
+    down = jnp.swapaxes(down, 3, 4)
+    tp = tp.T
     CP = round_up(C, LANES)
     piece = round_up(-(-(9 * C // 2 + 3 * rank) // B), 16)
     dims = (B, R, rows, width, C, rank, piece)

time: 63.9 us -> 65.5 us (1.025)
  Pallas kernels: 54.5 us -> 58.8 us
  local copies, waits for them, and re-layouts: 8.26 us -> 5.56 us
    pallas_call x1, Pallas kernels: 54.5 us -> 58.8 us  [block(): pl.pallas_call(functools.partial(kernel, dims), out_shape=jax.ShapeDtypeS...]
    unnamed x19 -> x13, local copies, waits for them, and re-layouts: 6.71 us -> 4.01 us
where the time goes in v2:
time: 65.5 us; the launch traced here: 65.1 us
  Pallas kernels  58.8 us (90%)
  local copies, waits for them, and re-layouts  5.56 us (8%)
  between operations  0.76 us (1%)
    pallas_call x1, Pallas kernels, block(): pl.pallas_call(functools.partial(kernel, dims), out_shape=jax.ShapeDtypeS...  58.8 us
    unnamed x13, local copies, waits for them, and re-layouts  4.01 us
    pallas_call x1, local copies, waits for them, and re-layouts, block(): pl.pallas_call(functools.partial(kernel, dims), out_shape=jax.ShapeDtypeS...  1.55 us

profile of v2, /device:TPU:1, one launch (start us, length us, event | category | flops | bytes accessed | tf_op | source)
XLA Modules:
  0.0 65.1 jit_solution(15922463953340511495)
XLA Ops:
  0.0 0.0 copy-start.2
  0.0 0.0 copy-start.3
  0.0 0.0 copy-start.5
  0.0 0.0 copy-start.4
  0.7 1.8 %copy.11.lat_ref = bf16[1,4,512,320]{3,2,1,0:T(8,128)(2,1)S(1)} copy(bf16[1,4,512,320]{2,3,1,0:T(8,128)(2,1)} %param.10) | data formatting | bytes 2621440 | tf_op args[0]
  2.6 0.0 copy-done.2
  2.6 0.0 copy-done.3
  2.6 0.0 copy-done.5
  2.6 0.0 copy-done.4
  2.6 0.0 copy-start
  2.6 1.1 %copy-done = bf16[1280,320]{0,1:T(8,128)(2,1)S(1)} copy-done((bf16[1280,320]{0,1:T(8,128)(2,1)S(1)}, bf16[1280,320]{0,1:T(8,128)(2,1)}, u32[]{:S(2)}) %copy-start) | copy-done | bytes 819224
  3.7 0.0 copy-start.1
  3.7 1.0 %copy-done.1 = bf16[1,3,3,320,64]{3,4,2,1,0:T(8,128)(2,1)S(1)} copy-done((bf16[1,3,3,320,64]{3,4,2,1,0:T(8,128)(2,1)S(1)}, bf16[1,3,3,320,64]{3,4,2,1,0:T(8,128)(2,1)}, u32[]{:S(2)}) %copy-start.1) | copy-done | bytes 368664
  4.8 58.8 %block.1 = bf16[1,4,512,320]{3,2,1,0:T(8,128)(2,1)S(1)} custom-call(bf16[1,4,512,320]{3,2,1,0:T(8,128)(2,1)S(1)} %copy.11.lat_ref, bf16[1,1280]{1,0:T(2,128)(2,1)S(1)} %copy-done.4, s32[1,1]{1,0:T(1,128)S(6)} %copy.13.ra_ref, s32[32]{0:T(128)S(1)} %copy-done.5, bf16[3,3,320,320]{3,2,1,0:T(8,128)(2,1)} %w1_hbm.1, bf16[1,3,3,64,320]{4,3,2,1,0:T(8,128)(2,1)S(1)} %bitcast.3, ...), custom_call_target="tpu_custom_call" | custom-call | tf_op jit(solution)/shard_map/block/pallas_call | solution.py:505
  63.6 1.6 %copy.12 = bf16[1,4,512,320]{2,3,1,0:T(8,128)(2,1)} copy(bf16[1,4,512,320]{3,2,1,0:T(8,128)(2,1)S(1)} %block.1) | data formatting | bytes 2621440 | tf_op jit(solution)/shard_map/block/pallas_call | solution.py:505
Async XLA Ops:
  0.0 2.6 %copy-start.2 = (bf16[384,384]{1,0:T(8,128)(2,1)S(1)}, bf16[384,384]{1,0:T(8,128)(2,1)}, u32[]{:S(2)}) copy-start(bf16[384,384]{1,0:T(8,128)(2,1)} %constant.2.clone.gg_ref) | copy-start | bytes 884740
  0.0 2.6 %copy-start.3 = (bf16[1,64,320]{2,1,0:T(8,128)(2,1)S(1)}, bf16[1,64,320]{2,1,0:T(8,128)(2,1)}, u32[]{:S(2)}) copy-start(bf16[1,64,320]{2,1,0:T(8,128)(2,1)} %up_hbm.1) | copy-start | bytes 122884
  0.0 2.6 %copy-start.5 = (s32[32]{0:T(128)S(1)}, s32[32]{0:T(128)}, u32[]{:S(2)}) copy-start(s32[32]{0:T(128)} %row_ref.1) | copy-start | bytes 388
  0.0 2.6 %copy-start.4 = (bf16[1,1280]{1,0:T(2,128)(2,1)S(1)}, bf16[1,1280]{1,0:T(2,128)(2,1)}, u32[]{:S(2)}) copy-start(bf16[1,1280]{1,0:T(2,128)(2,1)} %temb_ref.1) | copy-start | bytes 7684
  2.6 1.1 %copy-start = (bf16[1280,320]{0,1:T(8,128)(2,1)S(1)}, bf16[1280,320]{0,1:T(8,128)(2,1)}, u32[]{:S(2)}) copy-start(bf16[1280,320]{0,1:T(8,128)(2,1)} %param.18) | copy-start | bytes 2457604
  3.7 1.0 %copy-start.1 = (bf16[1,3,3,320,64]{3,4,2,1,0:T(8,128)(2,1)S(1)}, bf16[1,3,3,320,64]{3,4,2,1,0:T(8,128)(2,1)}, u32[]{:S(2)}) copy-start(bf16[1,3,3,320,64]{3,4,2,1,0:T(8,128)(2,1)} %param.15) | copy-start | bytes 1105924

commit v3 on v2

--- a/solution.py
+++ b/solution.py
@@ -89,11 +89,11 @@
     flat = packed
     total_rows = half + 3 * rank
     zero64 = jnp.zeros((rank, 64), BF16)
-    tap = [down[t // 3, t % 3].astype(F32).T.astype(BF16) for t in range(9)]
     for start in range(0, half, 160):
         t0, c0 = start // C, start % C
         t1, c1 = (start + half) // C, (start + half) % C
-        flat[pl.ds(start, 160), :] = jnp.concatenate([tap[t0][c0:c0 + 160], tap[t1][c1:c1 + 160]], axis=1)
+        flat[pl.ds(start, 160), :] = jnp.concatenate(
+            [down[t0 // 3, t0 % 3, pl.ds(c0, 160), :], down[t1 // 3, t1 % 3, pl.ds(c1, 160), :]], axis=1)
     flat[pl.ds(half, rank), :] = up[:, 0:128]
     flat[pl.ds(half + rank, rank), :] = up[:, 128:256]
     flat[pl.ds(half + 2 * rank, rank), :] = jnp.concatenate([up[:, 256:320], zero64], axis=1)
@@ -142,30 +142,30 @@
             device_id={"req": req(e)}, device_id_type=MESH))
         slot_copies[-1].start()
 
-    def up_copy():
-        return pltpu.make_async_remote_copy(
-            src_ref=lat.at[1], dst_ref=lat.at[rows + 1], send_sem=has.at[0], recv_sem=har.at[0],
-            device_id={"band": lax.rem(me + B - 1, B)}, device_id_type=MESH)
-
-    def down_copy():
-        return pltpu.make_async_remote_copy(
-            src_ref=lat.at[rows], dst_ref=lat.at[0], send_sem=has.at[1], recv_sem=har.at[1],
-            device_id={"band": band(1)}, device_id_type=MESH)
-
-    @pl.when(me > 0)
-    def _():
-        up_copy().start()
-
-    @pl.when(me < B - 1)
-    def _():
-        down_copy().start()
-
     p1_copies = []
     for d in range(1, B):
         p1_copies.append(pltpu.make_async_remote_copy(
             src_ref=packed.at[pl.ds(pl.multiple_of(band(d) * piece, 16), piece)], dst_ref=recv1.at[d],
             send_sem=p1s.at[d], recv_sem=p1r.at[d], device_id={"band": band(d)}, device_id_type=MESH))
         p1_copies[-1].start()
+
+    def up_copy():
+        return pltpu.make_async_remote_copy(
+            src_ref=lat.at[1], dst_ref=lat.at[rows + 1], send_sem=has.at[0], recv_sem=har.at[0],
+            device_id={"band": lax.rem(me + B - 1, B)}, device_id_type=MESH)
+
+    def down_copy():
+        return pltpu.make_async_remote_copy(
+            src_ref=lat.at[rows], dst_ref=lat.at[0], send_sem=has.at[1], recv_sem=har.at[1],
+            device_id={"band": band(1)}, device_id_type=MESH)
+
+    @pl.when(me > 0)
+    def _():
+        up_copy().start()
+
+    @pl.when(me < B - 1)
+    def _():
+        down_copy().start()
 
     ld[3].wait()
     t = temb_ref[...].astype(F32)
@@ -478,7 +478,6 @@
     B, R = mesh_shape["band"], mesh_shape["req"]
     _, rows, width, C = lat.shape
     rank = up.shape[1]
-    down = jnp.swapaxes(down, 3, 4)
     tp = tp.T
     CP = round_up(C, LANES)
     piece = round_up(-(-(9 * C // 2 + 3 * rank) // B), 16)

time: 65.5 us -> 61.7 us (0.942)
  Pallas kernels: 58.8 us -> 52.8 us
  local copies, waits for them, and re-layouts: 5.56 us -> 7.86 us
    pallas_call x1, Pallas kernels: 58.8 us -> 52.8 us  [block(): pl.pallas_call(functools.partial(kernel, dims), out_shape=jax.ShapeDtypeS...]
    unnamed x13 -> x14, local copies, waits for them, and re-layouts: 4.01 us -> 6.31 us
where the time goes in v3:
time: 61.7 us; the launch traced here: 61.4 us
  Pallas kernels  52.8 us (86%)
  local copies, waits for them, and re-layouts  7.86 us (13%)
  between operations  0.71 us (1%)
    pallas_call x1, Pallas kernels, block(): pl.pallas_call(functools.partial(kernel, dims), out_shape=jax.ShapeDtypeS...  52.8 us
    unnamed x14, local copies, waits for them, and re-layouts  6.31 us
    pallas_call x1, local copies, waits for them, and re-layouts, block(): pl.pallas_call(functools.partial(kernel, dims), out_shape=jax.ShapeDtypeS...  1.55 us

profile of v3, /device:TPU:1, one launch (start us, length us, event | category | flops | bytes accessed | tf_op | source)
XLA Modules:
  0.0 61.4 jit_solution(10571987100299767973)
XLA Ops:
  0.7 2.2 %copy.12.down_hbm = bf16[1,3,3,320,64]{4,3,2,1,0:T(8,128)(2,1)} copy(bf16[1,3,3,320,64]{3,4,2,1,0:T(8,128)(2,1)} %param.15) | data formatting | bytes 737280 | tf_op args[5]
  2.8 0.0 copy-start.2
  2.8 0.0 copy-start.3
  2.8 0.0 copy-start.4
  2.8 0.0 copy-start.5
  2.8 1.9 %copy.11.lat_ref = bf16[1,4,512,320]{3,2,1,0:T(8,128)(2,1)S(1)} copy(bf16[1,4,512,320]{2,3,1,0:T(8,128)(2,1)} %param.10) | data formatting | bytes 2621440 | tf_op args[0]
  4.7 0.0 copy-done.2
  4.7 0.0 copy-done.3
  4.7 0.0 copy-done.4
  4.7 0.0 copy-done.5
  4.8 0.0 copy-start
  4.8 1.1 %copy-done = bf16[1,3,3,320,64]{4,3,2,1,0:T(8,128)(2,1)S(1)} copy-done((bf16[1,3,3,320,64]{4,3,2,1,0:T(8,128)(2,1)S(1)}, bf16[1,3,3,320,64]{4,3,2,1,0:T(8,128)(2,1)}, u32[]{:S(2)}) %copy-start) | copy-done | bytes 368664
  5.9 0.0 copy-start.1
  5.9 1.1 %copy-done.1 = bf16[1280,320]{0,1:T(8,128)(2,1)S(1)} copy-done((bf16[1280,320]{0,1:T(8,128)(2,1)S(1)}, bf16[1280,320]{0,1:T(8,128)(2,1)}, u32[]{:S(2)}) %copy-start.1) | copy-done | bytes 819224
  7.0 52.8 %block.1 = bf16[1,4,512,320]{3,2,1,0:T(8,128)(2,1)S(1)} custom-call(bf16[1,4,512,320]{3,2,1,0:T(8,128)(2,1)S(1)} %copy.11.lat_ref, bf16[1,1280]{1,0:T(2,128)(2,1)S(1)} %copy-done.4, s32[1,1]{1,0:T(1,128)S(6)} %copy.14.ra_ref, s32[32]{0:T(128)S(1)} %copy-done.5, bf16[3,3,320,320]{3,2,1,0:T(8,128)(2,1)} %w1_hbm.1, bf16[1,3,3,320,64]{4,3,2,1,0:T(8,128)(2,1)S(1)} %copy-done, ...), custom_call_target="tpu_custom_call" | custom-call | tf_op jit(solution)/shard_map/block/pallas_call | solution.py:504
  59.9 1.6 %copy.13 = bf16[1,4,512,320]{2,3,1,0:T(8,128)(2,1)} copy(bf16[1,4,512,320]{3,2,1,0:T(8,128)(2,1)S(1)} %block.1) | data formatting | bytes 2621440 | tf_op jit(solution)/shard_map/block/pallas_call | solution.py:504
Async XLA Ops:
  2.8 1.9 %copy-start.2 = (bf16[384,384]{1,0:T(8,128)(2,1)S(1)}, bf16[384,384]{1,0:T(8,128)(2,1)}, u32[]{:S(2)}) copy-start(bf16[384,384]{1,0:T(8,128)(2,1)} %constant.2.clone.gg_ref) | copy-start | bytes 884740
  2.8 1.9 %copy-start.3 = (bf16[1,64,320]{2,1,0:T(8,128)(2,1)S(1)}, bf16[1,64,320]{2,1,0:T(8,128)(2,1)}, u32[]{:S(2)}) copy-start(bf16[1,64,320]{2,1,0:T(8,128)(2,1)} %up_hbm.1) | copy-start | bytes 122884
  2.8 1.9 %copy-start.4 = (bf16[1,1280]{1,0:T(2,128)(2,1)S(1)}, bf16[1,1280]{1,0:T(2,128)(2,1)}, u32[]{:S(2)}) copy-start(bf16[1,1280]{1,0:T(2,128)(2,1)} %temb_ref.1) | copy-start | bytes 7684
  2.8 1.9 %copy-start.5 = (s32[32]{0:T(128)S(1)}, s32[32]{0:T(128)}, u32[]{:S(2)}) copy-start(s32[32]{0:T(128)} %row_ref.1) | copy-start | bytes 388
  4.8 1.1 %copy-start = (bf16[1,3,3,320,64]{4,3,2,1,0:T(8,128)(2,1)S(1)}, bf16[1,3,3,320,64]{4,3,2,1,0:T(8,128)(2,1)}, u32[]{:S(2)}) copy-start(bf16[1,3,3,320,64]{4,3,2,1,0:T(8,128)(2,1)} %copy.12.down_hbm) | copy-start | bytes 1105924
  5.9 1.1 %copy-start.1 = (bf16[1280,320]{0,1:T(8,128)(2,1)S(1)}, bf16[1280,320]{0,1:T(8,128)(2,1)}, u32[]{:S(2)}) copy-start(bf16[1280,320]{0,1:T(8,128)(2,1)} %param.18) | copy-start | bytes 2457604
